TPU v7x, 32 devices: a whole 2x2x4 slice. The times are simulated.
32 devices in a mesh: blk: 8 (over z, core), fsdp: 4 (over y, x).
Axes of the slice: x: 2, y: 2, z: 4, core: 2. Of those that a mesh axis runs over, the one named last changes fastest.
Arguments:
- context: bfloat16 [8, 512, 2048], P('blk', 'fsdp'), may hold values from -6 to 6
- hidden: bfloat16 [8, 512, 4096], P('blk', 'fsdp'), may hold values from -6 to 6
- cotangent: bfloat16 [8, 512, 4096], P('blk', 'fsdp'), may hold values from -6 to 6
- gain: float32 [8, 4096], P('blk'), may hold values from 0.3 to 3
- weight: bfloat16 [8, 2048, 4096], P('blk', None, 'fsdp'), may hold values from -6 to 6
- step_counts: int32 [8], P('blk'), may hold values from 1 to 256
Outputs:
- new_weight: bfloat16 [8, 2048, 4096], P('blk', None, 'fsdp')
All inputs are finite; a program needn't handle non-finite values.
Results may differ from a plain program's by a relative error of at most 0.0038.
Values may be sent and summed in bfloat16 or wider, within the bound.
A program may use at most 64 MiB of HBM per device.

v0:
```python
import math
import jax
import jax.numpy as jnp
from jax import lax
from jax.sharding import PartitionSpec as P


def passed_along(block, axis, distance):
    devices = range(lax.axis_size(axis))
    route = [((i - distance) % len(devices), i) for i in devices]
    return lax.ppermute(block, axis, route)


def body(context, hidden, cotangent, gain, weight, step_counts):
    inputs = context[0]
    own = weight[0]
    width = inputs.shape[1]
    group = lax.axis_size("fsdp")
    rows = inputs.shape[0] * group
    scale = 1.0 / math.sqrt(width)
    rate = 0.5 * math.sqrt(width / rows)
    counts_wire = step_counts.astype(jnp.bfloat16)
    low_weight, low_count = passed_along((weight, counts_wire), "blk", 1)
    high_weight, high_count = passed_along((weight, counts_wire), "blk", -1)
    gathered = lax.all_gather(inputs, "fsdp", axis=0, tiled=True)
    branch = (jnp.dot(gathered, own, preferred_element_type=jnp.float32) * scale).astype(
        jnp.bfloat16
    )
    branch_rows = lax.all_to_all(branch, "fsdp", split_axis=0, concat_axis=1, tiled=True)
    residual_out = hidden[0].astype(jnp.float32) + branch_rows.astype(jnp.float32)
    inv_rms = lax.rsqrt(jnp.mean(residual_out * residual_out, axis=-1, keepdims=True) + 1e-05)
    scaled = gain[0][None, :] * cotangent[0].astype(jnp.float32)
    cross = jnp.mean(scaled * residual_out, axis=-1, keepdims=True)
    grad_rows = (inv_rms * scaled - residual_out * inv_rms**3 * cross).astype(jnp.bfloat16)
    out_grad = lax.all_to_all(grad_rows, "fsdp", split_axis=1, concat_axis=0, tiled=True)
    grad = (
        lax.dot_general(
            gathered, out_grad, (((0,), (0,)), ((), ())), preferred_element_type=jnp.float32
        )
        * scale
    )
    lower_c = low_count.astype(jnp.float32)[0]
    own_c = step_counts.astype(jnp.float32)[0]
    upper_c = high_count.astype(jnp.float32)[0]
    total = lower_c + own_c + upper_c
    mixed = (
        lower_c * low_weight[0].astype(jnp.float32)
        + own_c * own.astype(jnp.float32)
        + upper_c * high_weight[0].astype(jnp.float32)
    ) / total
    return (mixed - rate * grad).astype(jnp.bfloat16)[None]


def solution(mesh):
    return jax.shard_map(
        body,
        mesh=mesh,
        in_specs=(
            P("blk", "fsdp", None),
            P("blk", "fsdp", None),
            P("blk", "fsdp", None),
            P("blk", None),
            P("blk", None, "fsdp"),
            P("blk"),
        ),
        out_specs=P("blk", None, "fsdp"),
        check_vma=False,
    )
```

profile of v0, /device:TPU:0, one launch (start us, length us, event | category | flops | bytes accessed | tf_op | source)
XLA Modules:
  0.0 136.4 jit_solution(17001051425902305718)
XLA Ops:
  6.5 0.0 all-gather.3.cloned.1.call-start
  6.5 0.7 all-gather.3.cloned.1.call-update
  7.3 6.4 %copy.7 = bf16[1,2048,1024]{1,2,0:T(8,128)(2,1)} copy(bf16[1,2048,1024]{2,1,0:T(8,128)(2,1)} %param.10) | data formatting | bytes 8388608 | tf_op args[4]
  13.7 4.5 %collective-permute-start.3 = (bf16[1,2048,1024]{1,2,0:T(8,128)(2,1)}, bf16[1,2048,1024]{1,2,0:T(8,128)(2,1)}, u32[]{:S(2)}, u32[]{:S(2)}) collective-permute-start(bf16[1,2048,1024]{1,2,0:T(8,128)(2,1)} %copy.7), channel_id=1, source_target_pairs={{4,0},{8,4},{12,8},{16,12},{20,16},{24,20},{28,24},{0,28},{5,1},{9... | collective-permute-start | bytes 12582920 | tf_op jit(solution)/shard_map/ppermute | solution.py:11
  18.2 0.0 collective-permute-start.1
  18.2 29.1 %all-gather.3.cloned.1.call-done = bf16[1,512,2048]{2,1,0:T(8,128)(2,1)} async-done(((bf16[1,128,2048]{2,1,0:T(8,128)(2,1)}), bf16[1,512,2048]{2,1,0:T(8,128)(2,1)}) %all-gather.3.cloned.1.call-update) | async-done | bytes 2097168 | tf_op jit(solution)/shard_map/all_gather | solution.py:25
  47.2 6.2 %multiply_convert_fusion = bf16[512,1024]{1,0:T(8,128)(2,1)} fusion(bf16[1,2048,1024]{2,1,0:T(8,128)(2,1)} %param.10, bf16[1,512,2048]{2,1,0:T(8,128)(2,1)} %all-gather.3.cloned.1.call-done), kind=kOutput, calls=%fused_computation.25 | convolution fusion | flops 2148532224 | bytes 7340032 | tf_op jit(solution)/shard_map/dot_general | solution.py:26
  53.4 0.0 copy-start.3
  53.4 3.6 %all-to-all-start = ((bf16[4,128,1024]{2,1,0:T(8,128)(2,1)}), bf16[4,128,1024]{2,1,0:T(8,128)(2,1)S(1)}, u32[]{:S(2)}, u32[]{:S(2)}) async-start(bf16[4,128,1024]{2,1,0:T(8,128)(2,1)} %bitcast.10), calls=%async_computation | async-start | bytes 2097152 | tf_op jit(solution)/shard_map/all_to_all | solution.py:29
  57.1 0.5 broadcast.54
  57.6 0.0 copy-done.3
  57.6 0.6 reduce.3
  58.2 2.7 %reshape.67 = f32[128,4,1024]{2,1,0:T(4,128)S(1)} reshape(bf16[1,128,4096]{2,1,0:T(8,128)(2,1)} %param.7) | data formatting | bytes 3145728 | tf_op jit(solution)/shard_map/convert_element_type | solution.py:30
  61.0 3.7 %reshape.66 = f32[128,4,1024]{2,1,0:T(4,128)} reshape(bf16[1,128,4096]{2,1,0:T(8,128)(2,1)} %param.8) | data formatting | bytes 3145728 | tf_op jit(solution)/shard_map/convert_element_type | solution.py:32
  64.7 6.3 %all-to-all-done = bf16[4,128,1024]{2,1,0:T(8,128)(2,1)S(1)} async-done(((bf16[4,128,1024]{2,1,0:T(8,128)(2,1)}), bf16[4,128,1024]{2,1,0:T(8,128)(2,1)S(1)}, u32[]{:S(2)}, u32[]{:S(2)}) %all-to-all-start) | async-done | bytes 1048608 | tf_op jit(solution)/shard_map/all_to_all | solution.py:29
  71.0 0.2 convert_bitcast_fusion
  71.2 0.0 copy-start.1
  71.2 0.0 copy-start.2
  71.2 0.2 copy.14
  71.5 1.0 copy-done.1
  72.5 0.3 copy-done.2
  72.8 0.0 copy-start
  72.8 0.7 multiply_reduce_fusion
  73.5 0.9 copy-done
  74.4 3.8 %fusion.9 = bf16[128,4,1024]{2,0,1:T(8,128)(2,1)} fusion(bf16[4,128,1024]{2,1,0:T(8,128)(2,1)S(1)} %all-to-all-done, f32[128,4,1024]{2,1,0:T(4,128)S(1)} %reshape.67, f32[128,4,1024]{2,1,0:T(4,128)S(1)} %copy-done, f32[128]{0:T(128)S(1)} %get-tuple-element.9, f32[128]{0:T(128)S(1)} %get-tuple-element.8, f32[4,1024]{1,0:T(4,128)S(1)} %mul.101, ...), kind=kLoop, calls=%fused_computation.14 | loop fusion | flops 4194304 | bytes 6309376 | tf_op jit(solution)/shard_map/convert_element_type | solution.py:34
  78.1 0.0 copy-start.4
  78.1 3.6 %all-to-all-start.1 = ((bf16[128,4,1024]{2,0,1:T(8,128)(2,1)}), bf16[128,4,1024]{2,0,1:T(8,128)(2,1)S(1)}, u32[]{:S(2)}, u32[]{:S(2)}) async-start(bf16[128,4,1024]{2,0,1:T(8,128)(2,1)} %fusion.9), calls=%async_computation.1 | async-start | bytes 2097152 | tf_op jit(solution)/shard_map/all_to_all | solution.py:35
  82.4 25.0 %collective-permute-start.2 = (bf16[1]{0:T(256)(128)(2,1)}, bf16[1]{0:T(256)(128)(2,1)}, u32[]{:S(2)}, u32[]{:S(2)}) collective-permute-start(bf16[1]{0:T(256)(128)(2,1)} %convert_element_type.66), channel_id=1, source_target_pairs={{4,0},{8,4},{12,8},{16,12},{20,16},{24,20},{28,24},{0,28},{5,1},{9... | collective-permute-start | bytes 14 | tf_op jit(solution)/shard_map/ppermute | solution.py:11
  107.5 0.8 collective-permute-start
  108.3 0.0 collective-permute-done.2
  108.9 3.3 %collective-permute-done = bf16[1]{0:T(256)(128)(2,1)} collective-permute-done((bf16[1]{0:T(256)(128)(2,1)}, bf16[1]{0:T(256)(128)(2,1)}, u32[]{:S(2)}, u32[]{:S(2)}) %collective-permute-start) | collective-permute-done | bytes 34 | tf_op jit(solution)/shard_map/ppermute | solution.py:11
  114.2 0.0 collective-permute-done.3
  114.2 0.0 collective-permute-done.1
  114.2 0.0 all-to-all-done.1
  114.2 0.0 copy-done.4
  114.2 9.0 %fusion.4 = bf16[1,2048,1024]{1,2,0:T(8,128)(2,1)} fusion(f32[]{:T(128)S(6)} %add.35, bf16[1,2048,1024]{1,2,0:T(8,128)(2,1)} %collective-permute-done.3, f32[]{:T(128)S(6)} %convert.10, bf16[1,2048,1024]{1,2,0:T(8,128)(2,1)} %copy.7, f32[]{:T(128)} %bitcast.2, bf16[1,2048,1024]{1,2,0:T(8,128)(2,1)} %collective-permute-done.1, f32[]{:T(128)S(6)} %convert.9, ...), kind=kOutput, calls=%fused_computation.7 | convolution fusion | flops 2172649472 | bytes 19922960 | tf_op jit(solution)/shard_map/dot_general | solution.py:37
  123.2 6.4 %copy.13 = bf16[1,2048,1024]{2,1,0:T(8,128)(2,1)} copy(bf16[1,2048,1024]{1,2,0:T(8,128)(2,1)} %fusion.4) | data formatting | bytes 8388608 | tf_op jit(solution)/shard_map/broadcast_in_dim | solution.py:51
  (2 shorter events, 0.0 us)
Async XLA Ops:
  6.5 40.7 %all-gather.3.cloned.1.call-start = ((), (), s32[]{:S(2)}) async-start(), calls=%async_computation.2 | async-start | bytes 2621440 | tf_op jit(solution)/shard_map/all_gather | solution.py:25
  13.7 100.5 %collective-permute-start.3 = (bf16[1,2048,1024]{1,2,0:T(8,128)(2,1)}, bf16[1,2048,1024]{1,2,0:T(8,128)(2,1)}, u32[]{:S(2)}, u32[]{:S(2)}) collective-permute-start(bf16[1,2048,1024]{1,2,0:T(8,128)(2,1)} %copy.7), channel_id=1, source_target_pairs={{4,0},{8,4},{12,8},{16,12},{20,16},{24,20},{28,24},{0,28},{5,1},{9... | collective-permute-start | bytes 12582920 | tf_op jit(solution)/shard_map/ppermute | solution.py:11
  18.2 96.0 %collective-permute-start.1 = (bf16[1,2048,1024]{1,2,0:T(8,128)(2,1)}, bf16[1,2048,1024]{1,2,0:T(8,128)(2,1)}, u32[]{:S(2)}, u32[]{:S(2)}) collective-permute-start(bf16[1,2048,1024]{1,2,0:T(8,128)(2,1)} %copy.7), channel_id=1, source_target_pairs={{28,0},{0,4},{4,8},{8,12},{12,16},{16,20},{20,24},{24,28},{29,1},{... | collective-permute-start | bytes 12582920 | tf_op jit(solution)/shard_map/ppermute | solution.py:11
  53.4 4.1 %copy-start.3 = (f32[1,4096]{1,0:T(1,128)S(1)}, f32[1,4096]{1,0:T(1,128)}, u32[]{:S(2)}) copy-start(f32[1,4096]{1,0:T(1,128)} %param.9) | copy-start | bytes 49156
  53.4 17.5 %all-to-all-start = ((bf16[4,128,1024]{2,1,0:T(8,128)(2,1)}), bf16[4,128,1024]{2,1,0:T(8,128)(2,1)S(1)}, u32[]{:S(2)}, u32[]{:S(2)}) async-start(bf16[4,128,1024]{2,1,0:T(8,128)(2,1)} %bitcast.10), calls=%async_computation | async-start | bytes 2097152 | tf_op jit(solution)/shard_map/all_to_all | solution.py:29
  71.2 1.2 copy-start.1
  71.2 1.5 %copy-start.2 = (bf16[1,128,4096]{2,1,0:T(8,128)(2,1)S(1)}, bf16[1,128,4096]{2,1,0:T(8,128)(2,1)}, u32[]{:S(2)}) copy-start(bf16[1,128,4096]{2,1,0:T(8,128)(2,1)} %param.8) | copy-start | bytes 3145732
  72.8 1.6 %copy-start = (f32[128,4,1024]{2,1,0:T(4,128)S(1)}, f32[128,4,1024]{2,1,0:T(4,128)}, u32[]{:S(2)}) copy-start(f32[128,4,1024]{2,1,0:T(4,128)} %reshape.66) | copy-start | bytes 6291460
  78.1 36.1 %copy-start.4 = (bf16[1,512,2048]{2,1,0:T(8,128)(2,1)S(1)}, bf16[1,512,2048]{2,1,0:T(8,128)(2,1)}, u32[]{:S(2)}) copy-start(bf16[1,512,2048]{2,1,0:T(8,128)(2,1)} %all-gather.3.cloned.1.call-done) | copy-start | bytes 6291460
  78.1 36.0 %all-to-all-start.1 = ((bf16[128,4,1024]{2,0,1:T(8,128)(2,1)}), bf16[128,4,1024]{2,0,1:T(8,128)(2,1)S(1)}, u32[]{:S(2)}, u32[]{:S(2)}) async-start(bf16[128,4,1024]{2,0,1:T(8,128)(2,1)} %fusion.9), calls=%async_computation.1 | async-start | bytes 2097152 | tf_op jit(solution)/shard_map/all_to_all | solution.py:35
  82.4 25.9 %collective-permute-start.2 = (bf16[1]{0:T(256)(128)(2,1)}, bf16[1]{0:T(256)(128)(2,1)}, u32[]{:S(2)}, u32[]{:S(2)}) collective-permute-start(bf16[1]{0:T(256)(128)(2,1)} %convert_element_type.66), channel_id=1, source_target_pairs={{4,0},{8,4},{12,8},{16,12},{20,16},{24,20},{28,24},{0,28},{5,1},{9... | collective-permute-start | bytes 14 | tf_op jit(solution)/shard_map/ppermute | solution.py:11
  107.5 4.7 %collective-permute-start = (bf16[1]{0:T(256)(128)(2,1)}, bf16[1]{0:T(256)(128)(2,1)}, u32[]{:S(2)}, u32[]{:S(2)}) collective-permute-start(bf16[1]{0:T(256)(128)(2,1)} %convert_element_type.66), channel_id=1, source_target_pairs={{28,0},{0,4},{4,8},{8,12},{12,16},{16,20},{20,24},{24,28},{29,1},{... | collective-permute-start | bytes 14 | tf_op jit(solution)/shard_map/ppermute | solution.py:11
Sparse Core Ops, SparseCore 0:
  9.2 38.0 all-gather.2
where the time goes:
time: 137 us; the launch traced here: 136 us
  waiting for transfers between devices  39.4 us (29%)
  starting transfers between devices  37.6 us (27%)
  local copies, waits for them, and re-layouts  22.2 us (16%)
  between operations  16.7 us (12%)
  matrix products  15.2 us (11%)
  other arithmetic  5.3 us (4%)
    ppermute x4, starting transfers between devices, passed_along(): return lax.ppermute(block, axis, route)  30.3 us
    all_gather x1, waiting for transfers between devices, body(): gathered = lax.all_gather(inputs, 'fsdp', axis=0, tiled=True)  29.1 us
    unnamed x12, local copies, waits for them, and re-layouts  9.12 us
    dot_general x1, matrix products, body(): lax.dot_general(gathered, out_grad, (((0,), (0,)), ((), ())), preferred_e...  8.97 us
    broadcast_in_dim x1, local copies, waits for them, and re-layouts, body(): return (mixed - rate * grad).astype(jnp.bfloat16)[None]  6.39 us
    all_to_all x1, waiting for transfers between devices, body(): lax.all_to_all(branch, 'fsdp', split_axis=0, concat_axis=1, tiled=True)  6.27 us
    dot_general x1, matrix products, body(): jnp.dot(gathered, own, preferred_element_type=jnp.float32) * scale  6.19 us
    convert_element_type x1, other arithmetic, body(): (inv_rms * scaled - residual_out * inv_rms ** 3 * cross).astype(jnp.bfloa...  3.78 us
  transfers between devices with their start and end apart: 7, of which 3 were waited for; matrix products, arithmetic and copies ran while one was open for 18% of the time, Pallas kernels for 0%

commit v1 on v0

--- a/solution.py
+++ b/solution.py
@@ -3,6 +3,7 @@
 import jax.numpy as jnp
 from jax import lax
 from jax.sharding import PartitionSpec as P
+from jax.lax import axis_index, axis_size, ppermute
 
 
 def passed_along(block, axis, distance):
@@ -12,6 +13,22 @@
 
 
 def body(context, hidden, cotangent, gain, weight, step_counts):
+
+    def edit_strips_all_for(frame_in, device_axis, k_dim):
+        w_next = axis_size(device_axis)
+        big = axis_index(device_axis)
+        d_next, mixed_arr = (w_next, big)
+        part_now, val = (frame_in, 1)
+        while val < d_next:
+            side_arr = ppermute(
+                part_now, device_axis, perm=[(dev, dev ^ val) for dev in range(d_next)]
+            )
+            e_next = jnp.concatenate([part_now, side_arr], axis=k_dim)
+            work_now = jnp.concatenate([side_arr, part_now], axis=k_dim)
+            part_now = jnp.where(mixed_arr & val == 0, e_next, work_now)
+            val = 2 * val
+        return part_now
+
     inputs = context[0]
     own = weight[0]
     width = inputs.shape[1]
@@ -22,7 +39,7 @@
     counts_wire = step_counts.astype(jnp.bfloat16)
     low_weight, low_count = passed_along((weight, counts_wire), "blk", 1)
     high_weight, high_count = passed_along((weight, counts_wire), "blk", -1)
-    gathered = lax.all_gather(inputs, "fsdp", axis=0, tiled=True)
+    gathered = edit_strips_all_for(inputs, "fsdp", 0)
     branch = (jnp.dot(gathered, own, preferred_element_type=jnp.float32) * scale).astype(
         jnp.bfloat16
     )

time: 137 us -> 127 us (0.927)
  starting transfers between devices: 37.6 us -> 52.9 us
  between operations: 16.7 us -> 3.33 us
  local copies, waits for them, and re-layouts: 22.2 us -> 9.42 us
  other arithmetic: 5.3 us -> 6.96 us
    ppermute x0 -> x2, waiting for transfers between devices: none -> 31.2 us  [edit_strips_all_for(): ppermute(part_now, device_axis, perm=[(dev, dev ^ val) for dev in range(d...]
    all_gather x1 -> x0, waiting for transfers between devices: 29.1 us -> none  [body(): gathered = lax.all_gather(inputs, 'fsdp', axis=0, tiled=True)]
    ppermute x4, starting transfers between devices: 30.3 us -> 40.7 us  [passed_along(): return lax.ppermute(block, axis, route)]
    unnamed x12 -> x17, local copies, waits for them, and re-layouts: 9.12 us -> 2.72 us
    broadcast_in_dim x1 -> x0, local copies, waits for them, and re-layouts: 6.39 us -> none  [body(): return (mixed - rate * grad).astype(jnp.bfloat16)[None]]
    ppermute x0 -> x2, starting transfers between devices: none -> 4.78 us  [edit_strips_all_for(): ppermute(part_now, device_axis, perm=[(dev, dev ^ val) for dev in range(d...]
    select_n x0 -> x1, other arithmetic: none -> 1.59 us  [edit_strips_all_for(): part_now = jnp.where(mixed_arr & val == 0, e_next, work_now)]
    all_to_all x1, waiting for transfers between devices: 6.27 us -> 4.71 us  [body(): lax.all_to_all(branch, 'fsdp', split_axis=0, concat_axis=1, tiled=True)]
  transfers between devices with their start and end apart: 7 -> 8, of which waited for: 3 -> 4; matrix products, arithmetic and copies ran while one was open for 18% -> 15% of each run, Pallas kernels for 0% -> 0%
where the time goes in v1:
time: 127 us
  starting transfers between devices  52.9 us (42%)
  waiting for transfers between devices  39.1 us (31%)
  matrix products  15 us (12%)
  local copies, waits for them, and re-layouts  9.42 us (7%)
  other arithmetic  6.96 us (5%)
  between operations  3.33 us (3%)
    ppermute x4, starting transfers between devices, passed_along(): return lax.ppermute(block, axis, route)  40.7 us
    ppermute x2, waiting for transfers between devices, edit_strips_all_for(): ppermute(part_now, device_axis, perm=[(dev, dev ^ val) for dev in range(d...  31.2 us
    dot_general x1, matrix products, body(): lax.dot_general(gathered, out_grad, (((0,), (0,)), ((), ())), preferred_e...  9.11 us
    dot_general x1, matrix products, body(): jnp.dot(gathered, own, preferred_element_type=jnp.float32) * scale  5.89 us
    ppermute x2, starting transfers between devices, edit_strips_all_for(): ppermute(part_now, device_axis, perm=[(dev, dev ^ val) for dev in range(d...  4.78 us
    all_to_all x1, waiting for transfers between devices, body(): lax.all_to_all(branch, 'fsdp', split_axis=0, concat_axis=1, tiled=True)  4.71 us
    all_to_all x1, starting transfers between devices, body(): lax.all_to_all(branch, 'fsdp', split_axis=0, concat_axis=1, tiled=True)  3.79 us
    convert_element_type x1, other arithmetic, body(): (inv_rms * scaled - residual_out * inv_rms ** 3 * cross).astype(jnp.bfloa...  3.77 us
  transfers between devices with their start and end apart: 8, of which 4 were waited for; matrix products, arithmetic and copies ran while one was open for 15% of the time, Pallas kernels for 0%

profile of v1, /device:TPU:0, one launch (start us, length us, event | category | flops | bytes accessed | tf_op | source)
XLA Modules:
  0.0 126.8 jit_solution(8952814256427994535)
XLA Ops:
  0.0 2.9 %collective-permute-start.4 = (bf16[128,2048]{1,0:T(8,128)(2,1)}, bf16[128,2048]{1,0:T(8,128)(2,1)S(1)}, u32[]{:S(2)}, u32[]{:S(2)}) collective-permute-start(bf16[128,2048]{1,0:T(8,128)(2,1)} %bitcast.67), channel_id=1, source_target_pairs={{0,1},{1,0},{2,3},{3,2},{4,5},{5,4},{6,7},{7,6},{8,9},{9,8},{10,11... | collective-permute-start | bytes 1572872 | tf_op jit(solution)/shard_map/ppermute | solution.py:23
  2.9 12.1 %collective-permute-done.4 = bf16[128,2048]{1,0:T(8,128)(2,1)S(1)} collective-permute-done((bf16[128,2048]{1,0:T(8,128)(2,1)}, bf16[128,2048]{1,0:T(8,128)(2,1)S(1)}, u32[]{:S(2)}, u32[]{:S(2)}) %collective-permute-start.4) | collective-permute-done | bytes 524320 | tf_op jit(solution)/shard_map/ppermute | solution.py:23
  15.1 1.6 %maximum_select_fusion.1 = bf16[256,2048]{1,0:T(8,128)(2,1)S(1)} fusion(bf16[128,2048]{1,0:T(8,128)(2,1)S(1)} %collective-permute-done.4, bf16[128,2048]{1,0:T(8,128)(2,1)} %bitcast.68, pred[]{:T(512)S(6)} %eq.7), kind=kLoop, calls=%fused_computation.24 | loop fusion | flops 4718592 | bytes 2097153 | tf_op jit(solution)/shard_map/jit(_where)/select_n | solution.py:28
  16.7 0.0 copy-start.3
  16.7 1.8 %collective-permute-start.5 = (bf16[256,2048]{1,0:T(8,128)(2,1)S(1)}, bf16[256,2048]{1,0:T(8,128)(2,1)S(1)}, u32[]{:S(2)}, u32[]{:S(2)}) collective-permute-start(bf16[256,2048]{1,0:T(8,128)(2,1)S(1)} %maximum_select_fusion.1), channel_id=1, source_target_pairs={{0,2},{1,3},{2,0},{3,1},{4,6},{5,7},{6,4},{7,5},{8,10},{9,11},{10,... | collective-permute-start | bytes 3145736 | tf_op jit(solution)/shard_map/ppermute | solution.py:23
  18.5 0.0 collective-permute-start.1
  18.5 3.5 %collective-permute-start.3 = (bf16[1,2048,1024]{2,1,0:T(8,128)(2,1)}, bf16[1,2048,1024]{2,1,0:T(8,128)(2,1)}, u32[]{:S(2)}, u32[]{:S(2)}) collective-permute-start(bf16[1,2048,1024]{2,1,0:T(8,128)(2,1)} %param.10), channel_id=1, source_target_pairs={{4,0},{8,4},{12,8},{16,12},{20,16},{24,20},{28,24},{0,28},{5,1},{9... | collective-permute-start | bytes 12582920 | tf_op jit(solution)/shard_map/ppermute | solution.py:12
  22.1 19.0 %collective-permute-done.5 = bf16[256,2048]{1,0:T(8,128)(2,1)S(1)} collective-permute-done((bf16[256,2048]{1,0:T(8,128)(2,1)S(1)}, bf16[256,2048]{1,0:T(8,128)(2,1)S(1)}, u32[]{:S(2)}, u32[]{:S(2)}) %collective-permute-start.5) | collective-permute-done | bytes 1048608 | tf_op jit(solution)/shard_map/ppermute | solution.py:23
  41.1 0.0 copy-start.6
  41.1 5.9 %multiply_convert_fusion = bf16[512,1024]{1,0:T(8,128)(2,1)} fusion(bf16[1,2048,1024]{2,1,0:T(8,128)(2,1)} %param.10, bf16[256,2048]{1,0:T(8,128)(2,1)S(1)} %collective-permute-done.5, bf16[256,2048]{1,0:T(8,128)(2,1)S(1)} %maximum_select_fusion.1, pred[]{:T(512)S(6)} %eq.6), kind=kOutput, calls=%fused_computation.23 | convolution fusion | flops 2157969408 | bytes 7340033 | tf_op jit(solution)/shard_map/dot_general | solution.py:43
  47.0 0.0 copy-done.3
  47.0 0.0 copy-done.6
  47.0 0.0 copy-start.5
  47.0 3.8 %all-to-all-start = ((bf16[4,128,1024]{2,1,0:T(8,128)(2,1)}), bf16[4,128,1024]{2,1,0:T(8,128)(2,1)S(1)}, u32[]{:S(2)}, u32[]{:S(2)}) async-start(bf16[4,128,1024]{2,1,0:T(8,128)(2,1)} %bitcast.10), calls=%async_computation | async-start | bytes 2097152 | tf_op jit(solution)/shard_map/all_to_all | solution.py:46
  50.8 0.5 broadcast.52
  51.3 0.0 copy-done.5
  51.3 0.7 reduce.3
  52.0 2.7 %reshape.67 = f32[128,4,1024]{2,1,0:T(4,128)S(1)} reshape(bf16[1,128,4096]{2,1,0:T(8,128)(2,1)} %param.7) | data formatting | bytes 3145728 | tf_op jit(solution)/shard_map/convert_element_type | solution.py:47
  54.7 3.7 %reshape.66 = f32[128,4,1024]{2,1,0:T(4,128)} reshape(bf16[1,128,4096]{2,1,0:T(8,128)(2,1)} %param.8) | data formatting | bytes 3145728 | tf_op jit(solution)/shard_map/convert_element_type | solution.py:49
  58.4 4.7 %all-to-all-done = bf16[4,128,1024]{2,1,0:T(8,128)(2,1)S(1)} async-done(((bf16[4,128,1024]{2,1,0:T(8,128)(2,1)}), bf16[4,128,1024]{2,1,0:T(8,128)(2,1)S(1)}, u32[]{:S(2)}, u32[]{:S(2)}) %all-to-all-start) | async-done | bytes 1048608 | tf_op jit(solution)/shard_map/all_to_all | solution.py:46
  63.2 0.2 convert_bitcast_fusion
  63.4 0.0 copy-start.1
  63.4 0.0 copy-start.2
  63.4 0.2 copy.10
  63.7 1.0 copy-done.1
  64.6 0.3 copy-done.2
  64.9 0.0 copy-start
  64.9 0.7 multiply_reduce_fusion
  65.6 0.9 copy-done
  66.5 3.8 %fusion.10 = bf16[128,4,1024]{2,0,1:T(8,128)(2,1)} fusion(bf16[4,128,1024]{2,1,0:T(8,128)(2,1)S(1)} %all-to-all-done, f32[128,4,1024]{2,1,0:T(4,128)S(1)} %reshape.67, f32[128,4,1024]{2,1,0:T(4,128)S(1)} %copy-done, f32[128]{0:T(128)S(1)} %get-tuple-element.9, f32[128]{0:T(128)S(1)} %get-tuple-element.8, f32[4,1024]{1,0:T(4,128)S(1)} %mul.98, ...), kind=kLoop, calls=%fused_computation.14 | loop fusion | flops 4194304 | bytes 6309376 | tf_op jit(solution)/shard_map/convert_element_type | solution.py:51
  70.3 0.0 copy-start.4
  70.3 0.0 copy-start.7
  70.3 3.6 %all-to-all-start.1 = ((bf16[128,4,1024]{2,0,1:T(8,128)(2,1)}), bf16[128,4,1024]{2,0,1:T(8,128)(2,1)S(1)}, u32[]{:S(2)}, u32[]{:S(2)}) async-start(bf16[128,4,1024]{2,0,1:T(8,128)(2,1)} %fusion.10), calls=%async_computation.1 | async-start | bytes 2097152 | tf_op jit(solution)/shard_map/all_to_all | solution.py:52
  74.6 36.2 %collective-permute-start.2 = (bf16[1]{0:T(256)(128)(2,1)}, bf16[1]{0:T(256)(128)(2,1)}, u32[]{:S(2)}, u32[]{:S(2)}) collective-permute-start(bf16[1]{0:T(256)(128)(2,1)} %convert_element_type.66), channel_id=1, source_target_pairs={{4,0},{8,4},{12,8},{16,12},{20,16},{24,20},{28,24},{0,28},{5,1},{9... | collective-permute-start | bytes 14 | tf_op jit(solution)/shard_map/ppermute | solution.py:12
  110.8 1.0 collective-permute-start
  111.8 0.0 collective-permute-done.2
  112.4 3.3 %collective-permute-done = bf16[1]{0:T(256)(128)(2,1)} collective-permute-done((bf16[1]{0:T(256)(128)(2,1)}, bf16[1]{0:T(256)(128)(2,1)}, u32[]{:S(2)}, u32[]{:S(2)}) %collective-permute-start) | collective-permute-done | bytes 34 | tf_op jit(solution)/shard_map/ppermute | solution.py:12
  117.6 0.0 all-to-all-done.1
  117.6 0.0 collective-permute-done.1
  117.6 0.0 collective-permute-done.3
  117.6 0.0 copy-done.4
  117.7 0.0 copy-done.7
  117.7 9.1 %fusion.5 = bf16[1,2048,1024]{2,1,0:T(8,128)(2,1)} fusion(f32[]{:T(128)S(6)} %add.35, bf16[1,2048,1024]{2,1,0:T(8,128)(2,1)} %collective-permute-done.3, f32[]{:T(128)S(6)} %convert.10, bf16[1,2048,1024]{2,1,0:T(8,128)(2,1)} %param.10, f32[]{:T(128)} %bitcast.2, bf16[1,2048,1024]{2,1,0:T(8,128)(2,1)} %collective-permute-done.1, f32[]{:T(128)S(6)} %convert.9, ...), kind=kOutput, calls=%fused_computation.7 | convolution fusion | flops 2182086656 | bytes 19922960 | tf_op jit(solution)/shard_map/dot_general | solution.py:54
  (2 shorter events, 0.0 us)
Async XLA Ops:
  0.0 15.1 %collective-permute-start.4 = (bf16[128,2048]{1,0:T(8,128)(2,1)}, bf16[128,2048]{1,0:T(8,128)(2,1)S(1)}, u32[]{:S(2)}, u32[]{:S(2)}) collective-permute-start(bf16[128,2048]{1,0:T(8,128)(2,1)} %bitcast.67), channel_id=1, source_target_pairs={{0,1},{1,0},{2,3},{3,2},{4,5},{5,4},{6,7},{7,6},{8,9},{9,8},{10,11... | collective-permute-start | bytes 1572872 | tf_op jit(solution)/shard_map/ppermute | solution.py:23
  16.7 30.3 %copy-start.3 = (bf16[256,2048]{1,0:T(8,128)(2,1)}, bf16[256,2048]{1,0:T(8,128)(2,1)S(1)}, u32[]{:S(2)}) copy-start(bf16[256,2048]{1,0:T(8,128)(2,1)S(1)} %maximum_select_fusion.1) | copy-start | bytes 3145732
  16.7 24.4 %collective-permute-start.5 = (bf16[256,2048]{1,0:T(8,128)(2,1)S(1)}, bf16[256,2048]{1,0:T(8,128)(2,1)S(1)}, u32[]{:S(2)}, u32[]{:S(2)}) collective-permute-start(bf16[256,2048]{1,0:T(8,128)(2,1)S(1)} %maximum_select_fusion.1), channel_id=1, source_target_pairs={{0,2},{1,3},{2,0},{3,1},{4,6},{5,7},{6,4},{7,5},{8,10},{9,11},{10,... | collective-permute-start | bytes 3145736 | tf_op jit(solution)/shard_map/ppermute | solution.py:23
  18.5 99.1 %collective-permute-start.1 = (bf16[1,2048,1024]{2,1,0:T(8,128)(2,1)}, bf16[1,2048,1024]{2,1,0:T(8,128)(2,1)}, u32[]{:S(2)}, u32[]{:S(2)}) collective-permute-start(bf16[1,2048,1024]{2,1,0:T(8,128)(2,1)} %param.10), channel_id=1, source_target_pairs={{28,0},{0,4},{4,8},{8,12},{12,16},{16,20},{20,24},{24,28},{29,1},{... | collective-permute-start | bytes 12582920 | tf_op jit(solution)/shard_map/ppermute | solution.py:12
  18.5 99.1 %collective-permute-start.3 = (bf16[1,2048,1024]{2,1,0:T(8,128)(2,1)}, bf16[1,2048,1024]{2,1,0:T(8,128)(2,1)}, u32[]{:S(2)}, u32[]{:S(2)}) collective-permute-start(bf16[1,2048,1024]{2,1,0:T(8,128)(2,1)} %param.10), channel_id=1, source_target_pairs={{4,0},{8,4},{12,8},{16,12},{20,16},{24,20},{28,24},{0,28},{5,1},{9... | collective-permute-start | bytes 12582920 | tf_op jit(solution)/shard_map/ppermute | solution.py:12
  41.1 5.9 %copy-start.6 = (bf16[256,2048]{1,0:T(8,128)(2,1)}, bf16[256,2048]{1,0:T(8,128)(2,1)S(1)}, u32[]{:S(2)}) copy-start(bf16[256,2048]{1,0:T(8,128)(2,1)S(1)} %collective-permute-done.5) | copy-start | bytes 3145732
  47.0 4.3 %copy-start.5 = (f32[1,4096]{1,0:T(1,128)S(1)}, f32[1,4096]{1,0:T(1,128)}, u32[]{:S(2)}) copy-start(f32[1,4096]{1,0:T(1,128)} %param.9) | copy-start | bytes 49156
  47.0 16.2 %all-to-all-start = ((bf16[4,128,1024]{2,1,0:T(8,128)(2,1)}), bf16[4,128,1024]{2,1,0:T(8,128)(2,1)S(1)}, u32[]{:S(2)}, u32[]{:S(2)}) async-start(bf16[4,128,1024]{2,1,0:T(8,128)(2,1)} %bitcast.10), calls=%async_computation | async-start | bytes 2097152 | tf_op jit(solution)/shard_map/all_to_all | solution.py:46
  63.4 1.2 copy-start.1
  63.4 1.5 %copy-start.2 = (bf16[1,128,4096]{2,1,0:T(8,128)(2,1)S(1)}, bf16[1,128,4096]{2,1,0:T(8,128)(2,1)}, u32[]{:S(2)}) copy-start(bf16[1,128,4096]{2,1,0:T(8,128)(2,1)} %param.8) | copy-start | bytes 3145732
  64.9 1.6 %copy-start = (f32[128,4,1024]{2,1,0:T(4,128)S(1)}, f32[128,4,1024]{2,1,0:T(4,128)}, u32[]{:S(2)}) copy-start(f32[128,4,1024]{2,1,0:T(4,128)} %reshape.66) | copy-start | bytes 6291460
  70.3 47.3 %copy-start.4 = (bf16[256,2048]{1,0:T(8,128)(2,1)S(1)}, bf16[256,2048]{1,0:T(8,128)(2,1)}, u32[]{:S(2)}) copy-start(bf16[256,2048]{1,0:T(8,128)(2,1)} %copy-done.3) | copy-start | bytes 3145732
  70.3 47.3 %copy-start.7 = (bf16[256,2048]{1,0:T(8,128)(2,1)S(1)}, bf16[256,2048]{1,0:T(8,128)(2,1)}, u32[]{:S(2)}) copy-start(bf16[256,2048]{1,0:T(8,128)(2,1)} %copy-done.6) | copy-start | bytes 3145732
  70.3 47.3 %all-to-all-start.1 = ((bf16[128,4,1024]{2,0,1:T(8,128)(2,1)}), bf16[128,4,1024]{2,0,1:T(8,128)(2,1)S(1)}, u32[]{:S(2)}, u32[]{:S(2)}) async-start(bf16[128,4,1024]{2,0,1:T(8,128)(2,1)} %fusion.10), calls=%async_computation.1 | async-start | bytes 2097152 | tf_op jit(solution)/shard_map/all_to_all | solution.py:52
  74.6 37.2 %collective-permute-start.2 = (bf16[1]{0:T(256)(128)(2,1)}, bf16[1]{0:T(256)(128)(2,1)}, u32[]{:S(2)}, u32[]{:S(2)}) collective-permute-start(bf16[1]{0:T(256)(128)(2,1)} %convert_element_type.66), channel_id=1, source_target_pairs={{4,0},{8,4},{12,8},{16,12},{20,16},{24,20},{28,24},{0,28},{5,1},{9... | collective-permute-start | bytes 14 | tf_op jit(solution)/shard_map/ppermute | solution.py:12
  110.8 4.9 %collective-permute-start = (bf16[1]{0:T(256)(128)(2,1)}, bf16[1]{0:T(256)(128)(2,1)}, u32[]{:S(2)}, u32[]{:S(2)}) collective-permute-start(bf16[1]{0:T(256)(128)(2,1)} %convert_element_type.66), channel_id=1, source_target_pairs={{28,0},{0,4},{4,8},{8,12},{12,16},{16,20},{20,24},{24,28},{29,1},{... | collective-permute-start | bytes 14 | tf_op jit(solution)/shard_map/ppermute | solution.py:12
